TPU v7x, 128 devices: a whole 4x4x4 slice. The times are simulated.
128 devices in a mesh: img: 8 (over z_lo, x), txt: 16 (over z_hi, y, core).
Axes of the slice: x: 4, y: 4, z: 4 (z_hi: 2, z_lo: 2; z = z_hi * 2 + z_lo), core: 2. Of those that a mesh axis runs over, the one named last changes fastest.
Arguments:
- images: bfloat16 [22528, 1152], P(('img', 'txt')), may hold values from -0.19921875 to 0.19921875
- texts: bfloat16 [22528, 1152], P(('txt', 'img')), may hold values from -0.19921875 to 0.19921875
- match: int32 [22528], P(('img', 'txt')), may hold values from 0 to 22527, as said below
- log_scale: float32 [], replicated, may hold values from 2 to 2.8
- bias: float32 [], replicated, may hold values from -11 to -8
Outputs:
- loss: float32 [], replicated
- image_grad: float32 [22528, 1152], P(('img', 'txt'))
- text_grad: float32 [22528, 1152], P(('txt', 'img'))
Inputs may be any that keep to these rules, and one draw needn't show every extreme that they name: match names every text exactly once.
All inputs are finite; a program needn't handle non-finite values.
Results may differ from a plain program's by a relative error of at most 0.0044.
Values may be sent and summed in bfloat16 or wider, within the bound.
A program may use at most 128 MiB of HBM per device.

v0:
```python
import jax
import jax.numpy as jnp
from jax import lax
from jax.sharding import PartitionSpec as P

EPS = 1e-06


def normalize(rows):
    return rows * lax.rsqrt(jnp.sum(rows * rows, axis=-1, keepdims=True) + EPS)


def body(images, texts, match, log_scale, bias):
    scale = jnp.exp(log_scale)
    own_rows = images.shape[0]
    u_full, back_image = jax.vjp(normalize, images.astype(jnp.float32))
    v_full, back_text = jax.vjp(normalize, texts.astype(jnp.float32))
    image_block = lax.all_gather(u_full.astype(jnp.bfloat16), "txt", axis=0, tiled=True)
    label_block = lax.all_gather(match, "txt", axis=0, tiled=True)
    text_block = lax.all_gather(v_full.astype(jnp.bfloat16), "img", axis=0, tiled=True)
    width = text_block.shape[0]
    col_start = lax.axis_index("txt") * width
    columns = col_start + jnp.arange(width, dtype=jnp.int32)
    logits = (
        scale
        * lax.dot_general(
            image_block, text_block, (((1,), (1,)), ((), ())), preferred_element_type=jnp.float32
        )
        + bias
    )
    positive = (label_block[:, None] == columns[None, :]).astype(jnp.float32)
    sign = 2.0 * positive - 1.0
    partial_loss = jnp.sum(jax.nn.softplus(-sign * logits))
    grads = (jax.nn.sigmoid(logits) - positive).astype(jnp.bfloat16)
    image_part = scale * jnp.dot(grads, text_block, preferred_element_type=jnp.float32)
    image_sum = lax.psum_scatter(image_part, "txt", scatter_dimension=0, tiled=True)
    text_part = scale * lax.dot_general(
        grads, image_block, (((0,), (0,)), ((), ())), preferred_element_type=jnp.float32
    )
    text_sum = lax.psum_scatter(text_part, "img", scatter_dimension=0, tiled=True)
    total = lax.psum(partial_loss, ("img", "txt"))
    batch_total = own_rows * lax.axis_size("img") * lax.axis_size("txt")
    loss = total / batch_total
    image_grad = back_image(image_sum)[0]
    text_grad = back_text(text_sum)[0]
    return (loss, image_grad, text_grad)


def solution(mesh):
    in_specs = (P(("img", "txt"), None), P(("txt", "img"), None), P(("img", "txt")), P(), P())
    out_specs = (P(), P(("img", "txt"), None), P(("txt", "img"), None))
    return jax.shard_map(body, mesh=mesh, in_specs=in_specs, out_specs=out_specs, check_vma=False)
```

profile of v0, /device:TPU:1, one launch (start us, length us, event | category | flops | bytes accessed | tf_op | source)
XLA Modules:
  0.0 382.0 jit_solution(8888175320777759016)
XLA Ops:
  7.2 0.0 all-gather.5.cloned.1.call-start
  7.2 1.2 fusion.9
  8.4 1.9 fusion.10
  10.3 0.0 all-gather.5.cloned.1.call-update
  10.3 0.0 all-gather.3.cloned.1.call-start
  10.3 1.2 fusion.6
  11.5 1.9 fusion.7
  13.4 0.0 all-gather.3.cloned.1.call-update
  13.4 0.0 reduce-scatter.5.cloned.1.call-start
  14.8 1.2 dynamic-slice
  16.7 0.9 dynamic-update-slice
  17.6 66.9 %all-reduce = s32[2816]{0:T(1024)S(1)} all-reduce(s32[2816]{0:T(1024)S(1)} %dynamic-update-slice), channel_id=1, replica_groups=mesh['img'=8,'txt'=16] {'txt'}, use_global_device_ids=true, to_apply=%add | all-reduce | flops 2816 | bytes 22528
  84.5 0.0 all-gather.5.cloned.1.call-done
  84.5 42.1 %all-gather.3.cloned.1.call-done = bf16[2816,1152]{1,0:T(8,128)(2,1)} async-done(((bf16[176,1152]{1,0:T(8,128)(2,1)}), bf16[2816,1152]{1,0:T(8,128)(2,1)}) %all-gather.3.cloned.1.call-update) | async-done | bytes 6488080 | tf_op jit(solution)/shard_map/all_gather | solution.py:18
  126.6 0.0 copy-start.2
  126.6 27.8 %fusion.4 = (bf16[2816,1408]{1,0:T(8,128)(2,1)S(1)}, f32[]{:T(128)}) fusion(s32[1408]{0:T(1024)S(1)} %iota_add_fusion, s32[2816]{0:T(1024)S(1)} %all-reduce, f32[]{:T(128)S(6)} %copy.10, bf16[2816,1152]{1,0:T(8,128)(2,1)} %all-gather.3.cloned.1.call-done, bf16[1408,1152]{1,0:T(8,128)(2,1)} %all-gather.5.cloned.1.call-done, f32[]{:T(128)S(6)} %exp.10), kind=kOutput, calls=%fused_computation.7 | convolution fusion | flops 9214492672 | bytes 17678860 | tf_op jit(solution)/shard_map/dot_general | solution.py:26
  154.4 0.0 copy-start.4
  154.4 3.1 copy-done.4
  157.4 0.0 copy-done.2
  157.4 0.0 copy-start.3
  157.4 13.5 %convolution_multiply_fusion.1 = f32[1408,1152]{1,0:T(8,128)} fusion(bf16[2816,1408]{1,0:T(8,128)(2,1)S(1)} %get-tuple-element.3, bf16[2816,1152]{1,0:T(8,128)(2,1)S(1)} %copy-done.2, f32[]{:T(128)S(6)} %exp.10), kind=kOutput, calls=%fused_computation.11 | convolution fusion | flops 9136816128 | bytes 20905988 | tf_op jit(solution)/shard_map/dot_general | solution.py:37
  170.9 0.0 reduce-scatter.5.cloned.1.call-update
  171.0 0.0 reduce-scatter.3.cloned.1.call-start
  171.0 0.0 copy-done.3
  171.0 15.7 %convolution_multiply_fusion = f32[2816,1152]{1,0:T(8,128)} fusion(bf16[2816,1408]{1,0:T(8,128)(2,1)} %copy-done.4, bf16[1408,1152]{1,0:T(8,128)(2,1)S(1)} %copy-done.3, f32[]{:T(128)S(6)} %exp.10), kind=kOutput, calls=%fused_computation.10 | convolution fusion | flops 9138438144 | bytes 24150020 | tf_op jit(solution)/shard_map/dot_general | solution.py:35
  186.8 0.0 copy-start
  186.8 0.0 copy-start.1
  186.8 0.0 reduce-scatter.3.cloned.1.call-update
  186.8 101.9 %psum.7 = f32[]{:T(128)} all-reduce(f32[]{:T(128)} %get-tuple-element.4), channel_id=1, replica_groups=mesh['img'=8,'txt'=16] {'img','txt'}, use_global_device_ids=true, to_apply=%region_3.4 | all-reduce | flops 1 | bytes 8 | tf_op jit(solution)/shard_map/psum | solution.py:41
  289.4 0.0 reduce-scatter.5.cloned.1.call-done
  289.4 0.0 copy-done
  289.4 1.3 fusion.11
  290.7 2.2 add_add_fusion
  293.0 77.8 %reduce-scatter.3.cloned.1.call-done = f32[176,1152]{1,0:T(8,128)} async-done(((f32[2816,1152]{1,0:T(8,128)}), f32[176,1152]{1,0:T(8,128)}) %reduce-scatter.3.cloned.1.call-update) | async-done | bytes 811024 | tf_op jit(solution)/shard_map/reduce_scatter | solution.py:36
  370.8 0.0 copy-done.1
  370.8 1.3 fusion.8
  372.1 2.2 add_add_fusion.1
  (6 shorter events, 0.0 us)
Async XLA Ops:
  7.2 77.3 %all-gather.5.cloned.1.call-start = ((), (), s32[]{:S(2)}) async-start(), calls=%async_computation.3 | async-start | bytes 3649536 | tf_op jit(solution)/shard_map/all_gather | solution.py:20
  10.3 116.3 %all-gather.3.cloned.1.call-start = ((), (), s32[]{:S(2)}) async-start(), calls=%async_computation.2 | async-start | bytes 6893568 | tf_op jit(solution)/shard_map/all_gather | solution.py:18
  13.4 276.0 %reduce-scatter.5.cloned.1.call-start = ((), (), s32[]{:S(2)}) async-start(), calls=%async_computation.5 | async-start | bytes 7299072 | tf_op jit(solution)/shard_map/reduce_scatter | solution.py:40
  126.6 30.9 %copy-start.2 = (bf16[2816,1152]{1,0:T(8,128)(2,1)S(1)}, bf16[2816,1152]{1,0:T(8,128)(2,1)}, u32[]{:S(2)}) copy-start(bf16[2816,1152]{1,0:T(8,128)(2,1)} %all-gather.3.cloned.1.call-done) | copy-start | bytes 19464196
  154.4 3.1 copy-start.4
  157.4 13.6 %copy-start.3 = (bf16[1408,1152]{1,0:T(8,128)(2,1)S(1)}, bf16[1408,1152]{1,0:T(8,128)(2,1)}, u32[]{:S(2)}) copy-start(bf16[1408,1152]{1,0:T(8,128)(2,1)} %all-gather.5.cloned.1.call-done) | copy-start | bytes 9732100
  171.0 199.8 %reduce-scatter.3.cloned.1.call-start = ((), (), s32[]{:S(2)}) async-start(), calls=%async_computation.4 | async-start | bytes 13787136 | tf_op jit(solution)/shard_map/reduce_scatter | solution.py:36
  186.8 102.6 %copy-start = (bf16[176,1152]{1,0:T(8,128)(2,1)S(1)}, bf16[176,1152]{1,0:T(8,128)(2,1)}, u32[]{:S(2)}) copy-start(bf16[176,1152]{1,0:T(8,128)(2,1)} %param.6) | copy-start | bytes 1216516
  186.8 184.0 %copy-start.1 = (bf16[176,1152]{1,0:T(8,128)(2,1)S(1)}, bf16[176,1152]{1,0:T(8,128)(2,1)}, u32[]{:S(2)}) copy-start(bf16[176,1152]{1,0:T(8,128)(2,1)} %param.5) | copy-start | bytes 1216516
Sparse Core Ops, SparseCore 0:
  10.4 46.3 all-gather.4
  59.7 66.8 all-gather.2
  171.1 73.2 reduce-scatter.4
  248.6 122.1 reduce-scatter.2
where the time goes:
time: 383 us; the launch traced here: 382 us
  blocking collectives  169 us (44%)
  waiting for transfers between devices  120 us (31%)
  matrix products  57 us (15%)
  between operations  17.6 us (5%)
  other arithmetic  13.2 us (3%)
  local copies, waits for them, and re-layouts  5.23 us (1%)
    psum x1, blocking collectives, body(): total = lax.psum(partial_loss, ('img', 'txt'))  102 us
    reduce_scatter x1, waiting for transfers between devices, body(): lax.psum_scatter(image_part, 'txt', scatter_dimension=0, tiled=True)  77.8 us
    unnamed x1, blocking collectives  66.9 us
    all_gather x1, waiting for transfers between devices, body(): lax.all_gather(u_full.astype(jnp.bfloat16), 'txt', axis=0, tiled=True)  42.1 us
    dot_general x1, matrix products, body(): lax.dot_general(image_block, text_block, (((1,), (1,)), ((), ())), prefer...  27.8 us
    dot_general x1, matrix products, body(): jnp.dot(grads, text_block, preferred_element_type=jnp.float32)  15.7 us
    dot_general x1, matrix products, body(): lax.dot_general(grads, image_block, (((0,), (0,)), ((), ())), preferred_e...  13.5 us
  transfers between devices with their start and end apart: 4, of which 2 were waited for; matrix products, arithmetic and copies ran while one was open for 6% of the time, Pallas kernels for 0%

commit v1 on v0

v1 whole, which is shorter than its diff:
```python
import functools

import jax
import jax.numpy as jnp
from jax import lax
from jax.experimental import pallas as pl
from jax.experimental.pallas import tpu as pltpu
from jax.sharding import PartitionSpec as P

EPS = 1e-06
ROWS = 176
D = 1152
HALF = 704
CUT = 96
LOG2E = 1.4426950408889634
LN2 = 0.6931471805599453
BATCH = 22528
MESH = pl.DeviceIdType.MESH
F32 = jnp.float32
BF16 = jnp.bfloat16

ORDER = (7, 5, 6, 4, 1, 2, 3, 0)
PLACE = {k: i for i, k in enumerate(ORDER)}


def other_row(k):
    return 352 * PLACE[k]


def same_row(k):
    return 352 * PLACE[k] + ROWS


def nt(a, b):
    return lax.dot_general(a, b, (((1,), (1,)), ((), ())), preferred_element_type=F32)


def nn(a, b):
    return lax.dot_general(a, b, (((1,), (0,)), ((), ())), preferred_element_type=F32)


def tn(a, b):
    return lax.dot_general(a, b, (((0,), (0,)), ((), ())), preferred_element_type=F32)


def kernel(
    ls_ref, bias_ref, img_ref, txt_ref, lab_ref,
    du_ref, dv_ref, loss_ref,
    u, v, g0, g1, labs, labb, acc, lossbuf,
    dvf, core_out, core_in, stage, recv,
    gs, gr, cs, cr, lsend, lrecv, rs, rr, ccs, ccr, ps, pr,
):
    im = lax.axis_index("img")
    tx = lax.axis_index("txt")
    x = im % 4
    z = (tx // 8) * 2 + im // 4
    y = (tx // 2) % 4
    c = tx % 2

    def dev(dx=0, dy=0, zz=None, dc=0):
        z2 = z if zz is None else zz
        return ((z2 % 2) * 4 + (x + dx) % 4, (z2 // 2) * 8 + ((y + dy) % 4) * 2 + (c + dc) % 2)

    zi = z + 1 - 2 * (z % 2)
    zt = 3 - z
    plus = (dev(dy=1), dev(dx=1))
    minus = (dev(dy=3), dev(dx=3))
    part = (dev(zz=zi), dev(zz=zt))
    core = dev(dc=1)

    group = []
    for dy, dz, k in ((1, 0, 1), (3, 0, 2), (0, 1, 3), (2, 0, 4), (1, 1, 5), (3, 1, 6), (2, 1, 7)):
        for dc in (0, 1):
            group.append((dev(dy=dy, zz=zi if dz else z, dc=dc), 2 * PLACE[k] + 1 - dc))
    group.append((core, 2 * PLACE[0]))

    barrier = pltpu.get_barrier_semaphore()
    partners = [d for d, _ in group] + [plus[1], minus[1], part[1]]
    for d in partners:
        pl.semaphore_signal(barrier, inc=1, device_id=d, device_id_type=MESH)

    def norm(ref):
        rows = ref[...].astype(F32)
        return (rows * lax.rsqrt(jnp.sum(rows * rows, axis=-1, keepdims=True) + EPS)).astype(BF16)

    u[pl.ds(same_row(0), ROWS), :] = norm(img_ref)
    v[pl.ds(0, ROWS), :] = norm(txt_ref)
    labs[2 * PLACE[0] + 1] = lab_ref[...]
    pl.semaphore_wait(barrier, len(partners))

    sent = []

    def copy(src, dst, ss, sr, d):
        return pltpu.make_async_remote_copy(
            src_ref=src, dst_ref=dst, send_sem=ss, recv_sem=sr, device_id=d, device_id_type=MESH
        )

    def start(cp):
        cp.start()
        sent.append(cp)

    def base(f, k):
        return same_row(k) if f == 0 else ROWS * k

    def piece(f, k, lo, n):
        return (u, v)[f].at[pl.ds(base(f, k) + lo, n), :]

    moves = (
        (0, 1, 0, CUT, plus),
        (0, 1, CUT, ROWS - CUT, plus),
        (0, 2, CUT, ROWS - CUT, minus),
        (0, 2, 0, CUT, minus),
        (0, 3, 0, ROWS, part),
        (1, 4, 0, CUT, plus),
        (2, 4, CUT, ROWS - CUT, minus),
        (3, 5, 0, ROWS, plus),
        (3, 6, 0, ROWS, minus),
        (4, 7, 0, CUT, part),
        (4, 7, CUT, ROWS - CUT, part),
    )

    def gcopy(f, i):
        a, b, lo, n, to = moves[i]
        return copy(piece(f, a, lo, n), piece(f, b, lo, n), gs.at[f, i], gr.at[f, i], to[f])

    def gstart(i):
        for f in (0, 1):
            start(gcopy(f, i))

    def gwait(i):
        for f in (0, 1):
            gcopy(f, i).wait_recv()

    def xcopy(k):
        return copy(
            u.at[pl.ds(same_row(k), ROWS), :], u.at[pl.ds(other_row(k), ROWS), :], cs.at[k], cr.at[k], core
        )

    for i in (0, 2, 4, 1, 3):
        gstart(i)
    for n, (d, slot) in enumerate(group):
        start(copy(labs.at[2 * PLACE[0] + 1], labs.at[slot], lsend.at[n], lrecv.at[n], d))
    start(xcopy(0))

    scale = jnp.exp(jnp.full((8, 128), ls_ref[0], F32))
    c1 = scale[0:1, 0:1] * LOG2E
    c0 = jnp.full((1, 1), bias_ref[0] * LOG2E, F32)
    acc[...] = jnp.zeros_like(acc)

    for n, (d, slot) in enumerate(group):
        copy(labs.at[2 * PLACE[0] + 1], labs.at[slot], lsend.at[n], lrecv.at[n], d).wait_recv()
    bases = []
    for dx, zz in ((0, z), (3, z), (1, z), (0, zt), (2, z), (3, zt), (1, zt), (2, zt)):
        i2, t2 = dev(dx=dx, zz=zz)
        bases.append((t2 * 8 + i2) * ROWS)
    for s in range(16):
        lab = labs[s]
        place = jnp.full((8, 128), -1, jnp.int32)
        for j, b in enumerate(bases):
            rel = lab - b
            place = jnp.where((rel >= 0) & (rel < ROWS), rel + ROWS * j, place)
        placef = place.astype(F32)
        first = jnp.broadcast_to(placef[0:1, :], (128, 128)).T
        second = jnp.broadcast_to(placef[1:2, :], (128, 128)).T
        labb[pl.ds(s * ROWS, 128), :] = first
        labb[pl.ds(s * ROWS + 128, 48), :] = second[0:48, :]

    gh = (g0, g1)

    def logits(row, h):
        rows = pl.ds(row, 352)
        s = nt(u[rows, :], v[h * HALF : (h + 1) * HALF, :])
        l2 = s * c1 + c0
        e = jnp.exp2(l2)
        t = 1.0 + e
        r = pl.reciprocal(t, approx=True)
        lb = labb[rows, :]
        lbw = jnp.concatenate([lb] * 5 + [lb[:, :64]], axis=1)
        col = (lax.broadcasted_iota(jnp.int32, (352, HALF), 1) + h * HALF).astype(F32)
        pos = lbw == col
        gh[h][rows, :] = (r * jnp.where(pos, -1.0, e)).astype(BF16)
        t3 = t.reshape(44, 8, HALF)
        p3 = jnp.where(pos, l2, 0.0).reshape(44, 8, HALF)
        total = -jnp.sum(p3, axis=0)
        for a in range(0, 44, 8):
            w = t3[a]
            for b in range(a + 1, min(a + 8, 44)):
                w = w * t3[b]
            total = total + jnp.log2(w)
        acc[...] += total

    def logits_span(first, count, h):
        @pl.loop(0, count)
        def _(i):
            logits(pl.multiple_of((first + i) * 352, 16), h)

    gwait(0)
    gstart(5)
    gwait(2)
    gstart(6)
    xcopy(0).wait_recv()
    gwait(4)
    gstart(7)
    gstart(8)
    gwait(1)
    gwait(3)
    for k in (1, 2, 3):
        start(xcopy(k))
    logits_span(PLACE[0], 1, 0)
    gwait(5)
    gstart(9)
    gwait(6)
    gstart(10)
    start(xcopy(4))
    for k in (1, 2, 3):
        xcopy(k).wait_recv()
    logits_span(PLACE[1], 3, 0)
    xcopy(4).wait_recv()
    logits_span(PLACE[4], 1, 0)
    gwait(7)
    start(xcopy(5))
    gwait(8)
    start(xcopy(6))
    xcopy(5).wait_recv()
    logits_span(PLACE[5], 1, 0)
    gwait(9)
    gwait(10)
    start(xcopy(7))
    xcopy(6).wait_recv()
    logits_span(PLACE[6], 1, 0)
    xcopy(7).wait_recv()
    logits_span(PLACE[7], 1, 0)
    logits_span(0, 8, 1)

    mine = jnp.broadcast_to(jnp.sum(acc[...]).reshape(1, 1), (8, 128))
    lossbuf[0] = mine
    y1 = 1 - 2 * (y % 2)
    x1 = 1 - 2 * (x % 2)
    pairs = (core, dev(dy=y1 + 4), dev(dy=4 - y1), dev(dx=x1 + 4), dev(dx=4 - x1), part[0], part[1])

    def pcopy(i):
        return copy(lossbuf.at[2 * i], lossbuf.at[2 * i + 1], ps.at[i], pr.at[i], pairs[i])

    def pnext(i):
        pcopy(i).wait_recv()
        lossbuf[2 * i + 2] = lossbuf[2 * i] + lossbuf[2 * i + 1]
        if i + 1 < 7:
            start(pcopy(i + 1))

    start(pcopy(0))

    rmoves = (
        (7, 7, 0, ROWS, part),
        (5, 5, 0, ROWS, minus),
        (6, 6, 0, ROWS, plus),
        (4, 4, 0, CUT, minus),
        (4, 4, CUT, ROWS - CUT, plus),
        (1, 1, 0, CUT, minus),
        (1, 1, CUT, ROWS - CUT, minus),
        (2, 2, 0, CUT, plus),
        (2, 2, CUT, ROWS - CUT, plus),
        (3, 3, 0, ROWS, part),
    )
    S7, S5, S6, S4A, S4B, S1A, S1B, S2A, S2B, S3 = range(10)

    def rcopy(f, i):
        k, _, lo, n, to = rmoves[i]
        sl = pl.ds(lo, n)
        return copy(stage.at[f, k - 1, sl, :], recv.at[f, k - 1, sl, :], rs.at[f, i], rr.at[f, i], to[f])

    def got(f, k, lo=0, n=ROWS):
        return recv[f, k - 1, lo : lo + n, :].astype(F32)

    def put(f, k, val, lo=0, n=ROWS):
        stage[f, k - 1, lo : lo + n, :] = val.astype(BF16)

    def ccopy(k):
        return copy(core_out.at[k], core_in.at[k], ccs.at[k], ccr.at[k], core)

    def du(row, n):
        rows = pl.ds(row, n)
        return nn(g0[rows, :], v[0:HALF, :]) + nn(g1[rows, :], v[HALF:, :])

    def du_step(k, nxt):
        if k is None:
            d = du(other_row(nxt), ROWS)
            core_out[nxt] = d.astype(BF16)
            start(ccopy(nxt))
            return None
        if nxt is None:
            d = du(same_row(k), ROWS)
        else:
            d = du(same_row(k), 352)
            core_out[nxt] = d[ROWS:].astype(BF16)
            start(ccopy(nxt))
        ccopy(k).wait_recv()
        return d[:ROWS] + core_in[k].astype(F32)

    def dv_half(h):
        @pl.loop(0, 4)
        def _(i):
            cols = pl.ds(pl.multiple_of(i * 256, 256), 256)
            dvf[:, cols] = tn(gh[h][...], u[:, cols])

        dvf[:, 1024:] = tn(gh[h][...], u[:, 1024:])

    def dvb(j):
        return dvf[j * ROWS : (j + 1) * ROWS, :]

    du_step(None, 7)
    pnext(0)
    put(0, 7, du_step(7, 5))
    start(rcopy(0, S7))
    pnext(1)
    put(0, 5, du_step(5, 6))
    start(rcopy(0, S5))
    pnext(2)
    put(0, 6, du_step(6, 4))
    start(rcopy(0, S6))
    pnext(3)

    dv_half(1)
    for k, i in ((7, S7), (5, S5), (6, S6)):
        put(1, k, dvb(k - 4))
        start(rcopy(1, i))
    pnext(4)

    rcopy(0, S7).wait_recv()
    put(0, 4, du_step(4, 1) + got(0, 7))
    start(rcopy(0, S4A))
    start(rcopy(0, S4B))
    pnext(5)
    rcopy(1, S7).wait_recv()
    put(1, 4, dvb(0) + got(1, 7))
    start(rcopy(1, S4A))
    start(rcopy(1, S4B))
    pnext(6)

    dv_half(0)

    d = du_step(1, 2)
    put(0, 1, d[CUT:], CUT, ROWS - CUT)
    start(rcopy(0, S1B))
    rcopy(0, S4A).wait_recv()
    put(0, 1, d[:CUT] + got(0, 4, 0, CUT), 0, CUT)
    start(rcopy(0, S1A))
    d = du_step(2, 3)
    put(0, 2, d[:CUT], 0, CUT)
    start(rcopy(0, S2A))
    rcopy(0, S4B).wait_recv()
    put(0, 2, d[CUT:] + got(0, 4, CUT, ROWS - CUT), CUT, ROWS - CUT)
    start(rcopy(0, S2B))

    rcopy(1, S4A).wait_recv()
    put(1, 1, dvb(1)[CUT:], CUT, ROWS - CUT)
    put(1, 1, dvb(1)[:CUT] + got(1, 4, 0, CUT), 0, CUT)
    start(rcopy(1, S1B))
    start(rcopy(1, S1A))
    rcopy(1, S4B).wait_recv()
    put(1, 2, dvb(2)[:CUT], 0, CUT)
    put(1, 2, dvb(2)[CUT:] + got(1, 4, CUT, ROWS - CUT), CUT, ROWS - CUT)
    start(rcopy(1, S2A))
    start(rcopy(1, S2B))
    rcopy(1, S5).wait_recv()
    rcopy(1, S6).wait_recv()
    put(1, 3, dvb(3) + got(1, 5) + got(1, 6))
    start(rcopy(1, S3))

    rcopy(0, S5).wait_recv()
    rcopy(0, S6).wait_recv()
    put(0, 3, du_step(3, 0) + got(0, 5) + got(0, 6))
    start(rcopy(0, S3))

    d = du_step(0, None)
    for i in (S1A, S1B, S2A, S2B, S3):
        rcopy(0, i).wait_recv()
    du_ref[...] = d + got(0, 1) + got(0, 2) + got(0, 3)
    for i in (S1A, S1B, S2A, S2B, S3):
        rcopy(1, i).wait_recv()
    dv_ref[...] = dvb(0) + got(1, 1) + got(1, 2) + got(1, 3)
    loss_ref[...] = lossbuf[14] * (LN2 / BATCH)

    for cp in sent:
        cp.wait_send()


def fused(log_scale, bias, images, texts, labels):
    vm = pl.BlockSpec(memory_space=pltpu.VMEM)
    sm = pl.BlockSpec(memory_space=pltpu.SMEM)
    dma = pltpu.SemaphoreType.DMA
    block = jax.ShapeDtypeStruct((ROWS, D), F32)
    return pl.pallas_call(
        kernel,
        out_shape=(block, block, jax.ShapeDtypeStruct((8, 128), F32)),
        in_specs=[sm, sm, vm, vm, vm],
        out_specs=(vm, vm, vm),
        scratch_shapes=[
            pltpu.VMEM((16 * ROWS, D), BF16),
            pltpu.VMEM((8 * ROWS, D), BF16),
            pltpu.VMEM((16 * ROWS, HALF), BF16),
            pltpu.VMEM((16 * ROWS, HALF), BF16),
            pltpu.VMEM((16, 8, 128), jnp.int32),
            pltpu.VMEM((16 * ROWS, 128), F32),
            pltpu.VMEM((8, HALF), F32),
            pltpu.VMEM((15, 8, 128), F32),
            pltpu.VMEM((HALF, D), F32),
            pltpu.VMEM((8, ROWS, D), BF16),
            pltpu.VMEM((8, ROWS, D), BF16),
            pltpu.VMEM((2, 7, ROWS, D), BF16),
            pltpu.VMEM((2, 7, ROWS, D), BF16),
            dma((2, 11)), dma((2, 11)),
            dma((8,)), dma((8,)),
            dma((15,)), dma((15,)),
            dma((2, 10)), dma((2, 10)),
            dma((8,)), dma((8,)),
            dma((7,)), dma((7,)),
        ],
        compiler_params=pltpu.CompilerParams(
            collective_id=0, has_side_effects=True, vmem_limit_bytes=60 << 20
        ),
        name="contrastive",
    )(log_scale, bias, images, texts, labels)


def back(rows, grad):
    rows = rows.astype(F32)
    inv = lax.rsqrt(jnp.sum(rows * rows, axis=-1, keepdims=True) + EPS)
    n = rows * inv
    return (grad - n * jnp.sum(n * grad, axis=-1, keepdims=True)) * inv


def body(images, texts, match, log_scale, bias):
    labels = jnp.pad(match, (0, 1024 - ROWS)).reshape(8, 128)
    du, dv, loss = fused(log_scale.reshape(1), bias.reshape(1), images, texts, labels)
    scale = jnp.exp(log_scale)
    return (loss[0, 0], back(images, scale * du), back(texts, scale * dv))


def solution(mesh):
    in_specs = (P(("img", "txt"), None), P(("txt", "img"), None), P(("img", "txt")), P(), P())
    out_specs = (P(), P(("img", "txt"), None), P(("txt", "img"), None))
    return jax.shard_map(body, mesh=mesh, in_specs=in_specs, out_specs=out_specs, check_vma=False)
```

time: 383 us -> 115 us (0.30)
  blocking collectives: 169 us -> 0 us
  waiting for transfers between devices: 120 us -> 0 us
  Pallas kernels: 0 us -> 104 us
  matrix products: 57 us -> 0 us
  between operations: 17.6 us -> 2.07 us
  other arithmetic: 13.2 us -> 5.45 us
    pallas_call x0 -> x1, Pallas kernels: none -> 104 us  [fused(): pl.pallas_call(kernel, out_shape=(block, block, jax.ShapeDtypeStruct((8,...]
    psum x1 -> x0, blocking collectives: 102 us -> none  [body(): total = lax.psum(partial_loss, ('img', 'txt'))]
    reduce_scatter x2 -> x0, waiting for transfers between devices: 77.8 us -> none  [the longest x1 77.8 us: body(): lax.psum_scatter(image_part, 'txt', scatter_dimension=0, tiled=True)]
    unnamed x1 -> x0, blocking collectives: 66.9 us -> none
    dot_general x3 -> x0, matrix products: 57 us -> none  [the longest x1 27.8 us: body(): lax.dot_general(image_block, text_block, (((1,), (1,)), ((), ())), prefer...]
    all_gather x2 -> x0, waiting for transfers between devices: 42.1 us -> none  [the longest x1 42.1 us: body(): lax.all_gather(u_full.astype(jnp.bfloat16), 'txt', axis=0, tiled=True)]
    unnamed x13 -> x12, local copies, waits for them, and re-layouts: 5.23 us -> 0.69 us
    add_any x2 -> x0, other arithmetic: 4.47 us -> none  [normalize(): return rows * lax.rsqrt(jnp.sum(rows * rows, axis=-1, keepdims=True) + EPS)]
  transfers between devices with their start and end apart: 4 -> 0, of which waited for: 2 -> 0; matrix products, arithmetic and copies ran while one was open for 6% -> 0% of each run, Pallas kernels for 0% -> 0%
where the time goes in v1:
time: 115 us; the launch traced here: 114 us
  Pallas kernels  104 us (90%)
  other arithmetic  5.45 us (5%)
  local copies, waits for them, and re-layouts  2.47 us (2%)
  between operations  2.07 us (2%)
    pallas_call x1, Pallas kernels, fused(): pl.pallas_call(kernel, out_shape=(block, block, jax.ShapeDtypeStruct((8,...  104 us

profile of v1, /device:TPU:1, one launch (start us, length us, event | category | flops | bytes accessed | tf_op | source)
XLA Modules:
  0.0 114.2 jit_solution(8266529133492043907)
XLA Ops:
  0.6 0.0 copy-start.1
  2.0 1.2 %fusion.10 = f32[176]{0:T(256)S(1)} fusion(bf16[176,1152]{1,0:T(8,128)(2,1)} %img_ref.1), kind=kLoop, calls=%fused_computation.14 | loop fusion | flops 608080 | bytes 406208 | tf_op jit(solution)/shard_map/reduce_sum | solution.py:427
  3.2 0.0 copy-done.1
  3.2 0.2 fusion.11
  3.4 0.0 copy-start.5
  3.4 0.7 copy-done.5
  4.0 0.6 pad_bitcast_fusion.lab_ref
  4.6 0.0 copy-start
  4.6 0.0 copy-start.2
  4.6 104.2 %contrastive.1 = (f32[176,1152]{1,0:T(8,128)}, f32[176,1152]{1,0:T(8,128)}, f32[8,128]{1,0:T(8,128)}) custom-call(f32[1]{0:T(128)} %bitcast.5.ls_ref, f32[1]{0:T(128)} %bitcast.6.bias_ref, bf16[176,1152]{1,0:T(8,128)(2,1)} %img_ref.1, bf16[176,1152]{1,0:T(8,128)(2,1)} %txt_ref.1, s32[8,128]{1,0:T(8,128)} %pad_bitcast_fusion.lab_ref), custom_call_target="tpu_custom_call" | custom-call | tf_op jit(solution)/shard_map/contrastive/pallas_call | solution.py:392
  108.8 1.2 %slice.3 = f32[1,1]{1,0:T(1,128)} slice(f32[8,128]{1,0:T(8,128)} %get-tuple-element.6), slice={[0:1], [0:1]} | slice | bytes 8 | tf_op jit(solution)/shard_map/slice | solution.py:436
  110.0 0.0 copy-done
  110.0 0.0 copy-done.2
  110.0 0.0 copy-start.4
  110.0 1.9 %fusion.4 = (f32[176]{0:T(256)S(1)}, f32[176]{0:T(256)S(1)}) fusion(bf16[176,1152]{1,0:T(8,128)(2,1)S(1)} %copy-done.2, f32[176,1152]{1,0:T(8,128)} %get-tuple-element.8, f32[176]{0:T(256)S(1)} %add_rsqrt_fusion, f32[]{:T(128)S(6)} %exp.3, f32[176,1152]{1,0:T(8,128)} %get-tuple-element.7, f32[176]{0:T(256)S(1)} %add_rsqrt_fusion.1, ...), kind=kLoop, calls=%fused_computation.8 | loop fusion | flops 2027168 | bytes 2435844 | tf_op jit(solution)/shard_map/reduce_sum | solution.py:429
  111.9 0.0 copy-done.4
  111.9 0.0 copy-start.3
  111.9 1.1 fusion.9
  113.0 0.0 copy-done.3
  113.0 1.1 fusion.6
  (2 shorter events, 0.0 us)
Async XLA Ops:
  0.6 2.6 %copy-start.1 = (bf16[176,1152]{1,0:T(8,128)(2,1)S(1)}, bf16[176,1152]{1,0:T(8,128)(2,1)}, u32[]{:S(2)}) copy-start(bf16[176,1152]{1,0:T(8,128)(2,1)} %txt_ref.1) | copy-start | bytes 1216516
  3.4 0.7 copy-start.5
  4.6 105.4 %copy-start = (bf16[176,1152]{1,0:T(8,128)(2,1)S(1)}, bf16[176,1152]{1,0:T(8,128)(2,1)}, u32[]{:S(2)}) copy-start(bf16[176,1152]{1,0:T(8,128)(2,1)} %img_ref.1) | copy-start | bytes 1216516
  4.6 105.4 %copy-start.2 = (bf16[176,1152]{1,0:T(8,128)(2,1)S(1)}, bf16[176,1152]{1,0:T(8,128)(2,1)}, u32[]{:S(2)}) copy-start(bf16[176,1152]{1,0:T(8,128)(2,1)} %txt_ref.1) | copy-start | bytes 1216516
  110.0 1.9 %copy-start.4 = (f32[176,1152]{1,0:T(8,128)S(1)}, f32[176,1152]{1,0:T(8,128)}, u32[]{:S(2)}) copy-start(f32[176,1152]{1,0:T(8,128)} %get-tuple-element.7) | copy-start | bytes 2433028
  111.9 1.1 %copy-start.3 = (f32[176,1152]{1,0:T(8,128)S(1)}, f32[176,1152]{1,0:T(8,128)}, u32[]{:S(2)}) copy-start(f32[176,1152]{1,0:T(8,128)} %get-tuple-element.8) | copy-start | bytes 2433028

commit v2 on v1

--- a/solution.py
+++ b/solution.py
@@ -19,7 +19,7 @@
 F32 = jnp.float32
 BF16 = jnp.bfloat16
 
-ORDER = (7, 5, 6, 4, 1, 2, 3, 0)
+ORDER = (7, 5, 6, 4, 3, 1, 2, 0)
 PLACE = {k: i for i, k in enumerate(ORDER)}
 
 
@@ -48,7 +48,7 @@
     du_ref, dv_ref, loss_ref,
     u, v, g0, g1, labs, labb, acc, lossbuf,
     dvf, core_out, core_in, stage, recv,
-    gs, gr, cs, cr, lsend, lrecv, rs, rr, ccs, ccr, ps, pr,
+    own, dvt, gs, gr, cs, cr, lsend, lrecv, rs, rr, ccs, ccr, ps, pr, ts, tr,
 ):
     im = lax.axis_index("img")
     tx = lax.axis_index("txt")
@@ -74,6 +74,10 @@
             group.append((dev(dy=dy, zz=zi if dz else z, dc=dc), 2 * PLACE[k] + 1 - dc))
     group.append((core, 2 * PLACE[0]))
 
+    labs[...] = jnp.zeros_like(labs)
+    labs[2 * PLACE[0] + 1, 0:1, :] = lab_ref[0:1, 0:128]
+    labs[2 * PLACE[0] + 1, 1:2, 0:48] = lab_ref[0:1, 128:ROWS]
+
     barrier = pltpu.get_barrier_semaphore()
     partners = [d for d, _ in group] + [plus[1], minus[1], part[1]]
     for d in partners:
@@ -84,8 +88,6 @@
         return (rows * lax.rsqrt(jnp.sum(rows * rows, axis=-1, keepdims=True) + EPS)).astype(BF16)
 
     u[pl.ds(same_row(0), ROWS), :] = norm(img_ref)
-    v[pl.ds(0, ROWS), :] = norm(txt_ref)
-    labs[2 * PLACE[0] + 1] = lab_ref[...]
     pl.semaphore_wait(barrier, len(partners))
 
     sent = []
@@ -136,10 +138,13 @@
             u.at[pl.ds(same_row(k), ROWS), :], u.at[pl.ds(other_row(k), ROWS), :], cs.at[k], cr.at[k], core
         )
 
-    for i in (0, 2, 4, 1, 3):
-        gstart(i)
     for n, (d, slot) in enumerate(group):
         start(copy(labs.at[2 * PLACE[0] + 1], labs.at[slot], lsend.at[n], lrecv.at[n], d))
+    for i in (0, 2, 4, 1, 3):
+        start(gcopy(0, i))
+    v[pl.ds(0, ROWS), :] = norm(txt_ref)
+    for i in (0, 2, 4, 1, 3):
+        start(gcopy(1, i))
     start(xcopy(0))
 
     scale = jnp.exp(jnp.full((8, 128), ls_ref[0], F32))
@@ -147,25 +152,8 @@
     c0 = jnp.full((1, 1), bias_ref[0] * LOG2E, F32)
     acc[...] = jnp.zeros_like(acc)
 
-    for n, (d, slot) in enumerate(group):
-        copy(labs.at[2 * PLACE[0] + 1], labs.at[slot], lsend.at[n], lrecv.at[n], d).wait_recv()
-    bases = []
-    for dx, zz in ((0, z), (3, z), (1, z), (0, zt), (2, z), (3, zt), (1, zt), (2, zt)):
-        i2, t2 = dev(dx=dx, zz=zz)
-        bases.append((t2 * 8 + i2) * ROWS)
-    for s in range(16):
-        lab = labs[s]
-        place = jnp.full((8, 128), -1, jnp.int32)
-        for j, b in enumerate(bases):
-            rel = lab - b
-            place = jnp.where((rel >= 0) & (rel < ROWS), rel + ROWS * j, place)
-        placef = place.astype(F32)
-        first = jnp.broadcast_to(placef[0:1, :], (128, 128)).T
-        second = jnp.broadcast_to(placef[1:2, :], (128, 128)).T
-        labb[pl.ds(s * ROWS, 128), :] = first
-        labb[pl.ds(s * ROWS + 128, 48), :] = second[0:48, :]
-
     gh = (g0, g1)
+    one = jnp.minimum(im + 1, 1)
 
     def logits(row, h):
         rows = pl.ds(row, 352)
@@ -190,7 +178,7 @@
         acc[...] += total
 
     def logits_span(first, count, h):
-        @pl.loop(0, count)
+        @pl.loop(0, count * one)
         def _(i):
             logits(pl.multiple_of((first + i) * 352, 16), h)
 
@@ -198,7 +186,24 @@
     gstart(5)
     gwait(2)
     gstart(6)
-    xcopy(0).wait_recv()
+    for n, (d, slot) in enumerate(group):
+        copy(labs.at[2 * PLACE[0] + 1], labs.at[slot], lsend.at[n], lrecv.at[n], d).wait_recv()
+    bases = []
+    for dx, zz in ((0, z), (3, z), (1, z), (0, zt), (2, z), (3, zt), (1, zt), (2, zt)):
+        i2, t2 = dev(dx=dx, zz=zz)
+        bases.append((t2 * 8 + i2) * ROWS)
+    for s in range(16):
+        lab = labs[s]
+        place = jnp.full((8, 128), -1, jnp.int32)
+        for j, b in enumerate(bases):
+            rel = lab - b
+            place = jnp.where((rel >= 0) & (rel < ROWS), rel + ROWS * j, place)
+        placef = place.astype(F32)
+        first = jnp.broadcast_to(placef[0:1, :], (128, 128)).T
+        second = jnp.broadcast_to(placef[1:2, :], (128, 128)).T
+        labb[pl.ds(s * ROWS, 128), :] = first
+        labb[pl.ds(s * ROWS + 128, 48), :] = second[0:48, :]
+
     gwait(4)
     gstart(7)
     gstart(8)
@@ -206,15 +211,17 @@
     gwait(3)
     for k in (1, 2, 3):
         start(xcopy(k))
+    xcopy(0).wait_recv()
     logits_span(PLACE[0], 1, 0)
+    for k in (1, 2, 3):
+        xcopy(k).wait_recv()
+    logits_span(PLACE[3], 1, 0)
     gwait(5)
     gstart(9)
     gwait(6)
     gstart(10)
     start(xcopy(4))
-    for k in (1, 2, 3):
-        xcopy(k).wait_recv()
-    logits_span(PLACE[1], 3, 0)
+    logits_span(PLACE[1], 2, 0)
     xcopy(4).wait_recv()
     logits_span(PLACE[4], 1, 0)
     gwait(7)
@@ -277,108 +284,169 @@
     def ccopy(k):
         return copy(core_out.at[k], core_in.at[k], ccs.at[k], ccr.at[k], core)
 
-    def du(row, n):
-        rows = pl.ds(row, n)
-        return nn(g0[rows, :], v[0:HALF, :]) + nn(g1[rows, :], v[HALF:, :])
-
-    def du_step(k, nxt):
-        if k is None:
-            d = du(other_row(nxt), ROWS)
-            core_out[nxt] = d.astype(BF16)
+    def du_block(k, nxt):
+        @pl.loop(0, one)
+        def _(_i):
+            first = other_row(nxt) if k is None else same_row(k)
+            n = ROWS if k is None or nxt is None else 352
+            rows = pl.ds(first, n)
+            d = nn(g0[rows, :], v[0:HALF, :]) + nn(g1[rows, :], v[HALF:, :])
+            if k is not None:
+                own[k] = d[:ROWS]
+            if nxt is not None:
+                core_out[nxt] = d[n - ROWS :].astype(BF16)
+
+        if nxt is not None:
             start(ccopy(nxt))
-            return None
-        if nxt is None:
-            d = du(same_row(k), ROWS)
-        else:
-            d = du(same_row(k), 352)
-            core_out[nxt] = d[ROWS:].astype(BF16)
-            start(ccopy(nxt))
-        ccopy(k).wait_recv()
-        return d[:ROWS] + core_in[k].astype(F32)
-
-    def dv_half(h):
-        @pl.loop(0, 4)
-        def _(i):
-            cols = pl.ds(pl.multiple_of(i * 256, 256), 256)
-            dvf[:, cols] = tn(gh[h][...], u[:, cols])
-
-        dvf[:, 1024:] = tn(gh[h][...], u[:, 1024:])
-
-    def dvb(j):
-        return dvf[j * ROWS : (j + 1) * ROWS, :]
-
-    du_step(None, 7)
+
+    def tcols(n):
+        return slice(256 * n, min(256 * n + 256, D))
+
+    tmoves = (
+        (7, 0, ROWS, part),
+        (5, 0, ROWS, minus),
+        (6, 0, ROWS, plus),
+        (3, 0, ROWS, part),
+        (1, CUT, ROWS - CUT, minus),
+        (2, 0, CUT, plus),
+    )
+    T7, T5, T6, T3, T1B, T2A = range(6)
+
+    def tcopy(i, n):
+        k, lo, rows, to = tmoves[i]
+        sl, cols = pl.ds(lo, rows), pl.ds(256 * n, min(256, D - 256 * n))
+        return copy(
+            stage.at[1, k - 1, sl, cols], recv.at[1, k - 1, sl, cols], ts.at[i, n], tr.at[i, n], to[1]
+        )
+
+    def twait(i):
+        for n in range(5):
+            tcopy(i, n).wait_recv()
+
+    def dv_late(n):
+        cols = tcols(n)
+
+        @pl.loop(0, one)
+        def _(_i):
+            d = tn(g1[...], u[:, cols])
+            dvt[:, cols] = d[0:ROWS]
+            for k in (5, 6, 7):
+                stage[1, k - 1, :, cols] = d[(k - 4) * ROWS : (k - 3) * ROWS].astype(BF16)
+
+        for i in (T7, T5, T6):
+            start(tcopy(i, n))
+
+    def dv_early(n):
+        cols = tcols(n)
+        for i in (T5, T6):
+            tcopy(i, n).wait_recv()
+
+        @pl.loop(0, one)
+        def _(_i):
+            d = tn(g0[...], u[:, cols])
+            dvf[:, cols] = d[0 : 3 * ROWS]
+            stage[1, 0, CUT:, cols] = d[ROWS + CUT : 2 * ROWS].astype(BF16)
+            stage[1, 1, 0:CUT, cols] = d[2 * ROWS : 2 * ROWS + CUT].astype(BF16)
+            both = recv[1, 4, :, cols].astype(F32) + recv[1, 5, :, cols].astype(F32)
+            stage[1, 2, :, cols] = (d[3 * ROWS :] + both).astype(BF16)
+
+        for i in (T3, T1B, T2A):
+            start(tcopy(i, n))
+
+    def mine_of(k, lo=0, n=ROWS):
+        return own[k, lo : lo + n, :] + core_in[k, lo : lo + n, :].astype(F32)
+
+    du_block(None, 7)
+    dv_late(0)
     pnext(0)
-    put(0, 7, du_step(7, 5))
+    du_block(7, 5)
+    ccopy(7).wait_recv()
+    put(0, 7, mine_of(7))
     start(rcopy(0, S7))
+    dv_late(1)
     pnext(1)
-    put(0, 5, du_step(5, 6))
+    du_block(5, 6)
+    ccopy(5).wait_recv()
+    put(0, 5, mine_of(5))
     start(rcopy(0, S5))
+    dv_late(2)
     pnext(2)
-    put(0, 6, du_step(6, 4))
+    du_block(6, 4)
+    ccopy(6).wait_recv()
+    put(0, 6, mine_of(6))
     start(rcopy(0, S6))
+    dv_late(3)
     pnext(3)
-
-    dv_half(1)
-    for k, i in ((7, S7), (5, S5), (6, S6)):
-        put(1, k, dvb(k - 4))
-        start(rcopy(1, i))
+    dv_late(4)
     pnext(4)
-
+    du_block(4, 3)
+    du_block(3, 1)
+    pnext(5)
+
+    ccopy(4).wait_recv()
     rcopy(0, S7).wait_recv()
-    put(0, 4, du_step(4, 1) + got(0, 7))
+    put(0, 4, mine_of(4) + got(0, 7))
     start(rcopy(0, S4A))
     start(rcopy(0, S4B))
-    pnext(5)
-    rcopy(1, S7).wait_recv()
-    put(1, 4, dvb(0) + got(1, 7))
+    twait(T7)
+    put(1, 4, dvt[...] + got(1, 7))
     start(rcopy(1, S4A))
     start(rcopy(1, S4B))
     pnext(6)
 
-    dv_half(0)
-
-    d = du_step(1, 2)
-    put(0, 1, d[CUT:], CUT, ROWS - CUT)
+    dv_early(0)
+    du_block(1, 2)
+    ccopy(1).wait_recv()
+    put(0, 1, mine_of(1, CUT, ROWS - CUT), CUT, ROWS - CUT)
     start(rcopy(0, S1B))
+    dv_early(1)
+    ccopy(3).wait_recv()
+    rcopy(0, S5).wait_recv()
+    rcopy(0, S6).wait_recv()
+    put(0, 3, mine_of(3) + got(0, 5) + got(0, 6))
+    start(rcopy(0, S3))
+    du_block(2, 0)
+    ccopy(2).wait_recv()
+    put(0, 2, mine_of(2, 0, CUT), 0, CUT)
+    start(rcopy(0, S2A))
+    dv_early(2)
+    dv_early(3)
+
     rcopy(0, S4A).wait_recv()
-    put(0, 1, d[:CUT] + got(0, 4, 0, CUT), 0, CUT)
+    put(0, 1, mine_of(1, 0, CUT) + got(0, 4, 0, CUT), 0, CUT)
     start(rcopy(0, S1A))
-    d = du_step(2, 3)
-    put(0, 2, d[:CUT], 0, CUT)
-    start(rcopy(0, S2A))
     rcopy(0, S4B).wait_recv()
-    put(0, 2, d[CUT:] + got(0, 4, CUT, ROWS - CUT), CUT, ROWS - CUT)
+    put(0, 2, mine_of(2, CUT, ROWS - CUT) + got(0, 4, CUT, ROWS - CUT), CUT, ROWS - CUT)
     start(rcopy(0, S2B))
-
+    dv_early(4)
     rcopy(1, S4A).wait_recv()
-    put(1, 1, dvb(1)[CUT:], CUT, ROWS - CUT)
-    put(1, 1, dvb(1)[:CUT] + got(1, 4, 0, CUT), 0, CUT)
-    start(rcopy(1, S1B))
+    put(1, 1, dvf[ROWS : ROWS + CUT, :] + got(1, 4, 0, CUT), 0, CUT)
     start(rcopy(1, S1A))
     rcopy(1, S4B).wait_recv()
-    put(1, 2, dvb(2)[:CUT], 0, CUT)
-    put(1, 2, dvb(2)[CUT:] + got(1, 4, CUT, ROWS - CUT), CUT, ROWS - CUT)
-    start(rcopy(1, S2A))
+    put(1, 2, dvf[2 * ROWS + CUT : 3 * ROWS, :] + got(1, 4, CUT, ROWS - CUT), CUT, ROWS - CUT)
     start(rcopy(1, S2B))
-    rcopy(1, S5).wait_recv()
-    rcopy(1, S6).wait_recv()
-    put(1, 3, dvb(3) + got(1, 5) + got(1, 6))
-    start(rcopy(1, S3))
-
-    rcopy(0, S5).wait_recv()
-    rcopy(0, S6).wait_recv()
-    put(0, 3, du_step(3, 0) + got(0, 5) + got(0, 6))
-    start(rcopy(0, S3))
-
-    d = du_step(0, None)
-    for i in (S1A, S1B, S2A, S2B, S3):
-        rcopy(0, i).wait_recv()
-    du_ref[...] = d + got(0, 1) + got(0, 2) + got(0, 3)
-    for i in (S1A, S1B, S2A, S2B, S3):
-        rcopy(1, i).wait_recv()
-    dv_ref[...] = dvb(0) + got(1, 1) + got(1, 2) + got(1, 3)
-    loss_ref[...] = lossbuf[14] * (LN2 / BATCH)
+    du_block(0, None)
+
+    ccopy(0).wait_recv()
+    loss_ref[0] = jnp.max(lossbuf[14]) * (LN2 / BATCH)
+
+    def finish(f, ref, out, grad):
+        rows = ref[...].astype(F32)
+        inv = lax.rsqrt(jnp.sum(rows * rows, axis=-1, keepdims=True) + EPS)
+        n = rows * inv
+        if f == 0:
+            for i in (S1A, S1B, S2A, S2B, S3):
+                rcopy(0, i).wait_recv()
+        else:
+            for i in (S1A, S2B):
+                rcopy(1, i).wait_recv()
+            for i in (T3, T1B, T2A):
+                twait(i)
+        grad = (grad + got(f, 1) + got(f, 2) + got(f, 3)) * scale[0:1, 0:1]
+        out[...] = (grad - n * jnp.sum(n * grad, axis=-1, keepdims=True)) * inv
+
+    finish(0, img_ref, du_ref, mine_of(0))
+    finish(1, txt_ref, dv_ref, dvf[0:ROWS, :])
 
     for cp in sent:
         cp.wait_send()
@@ -391,9 +459,9 @@
     block = jax.ShapeDtypeStruct((ROWS, D), F32)
     return pl.pallas_call(
         kernel,
-        out_shape=(block, block, jax.ShapeDtypeStruct((8, 128), F32)),
+        out_shape=(block, block, jax.ShapeDtypeStruct((1,), F32)),
         in_specs=[sm, sm, vm, vm, vm],
-        out_specs=(vm, vm, vm),
+        out_specs=(vm, vm, sm),
         scratch_shapes=[
             pltpu.VMEM((16 * ROWS, D), BF16),
             pltpu.VMEM((8 * ROWS, D), BF16),
@@ -403,17 +471,20 @@
             pltpu.VMEM((16 * ROWS, 128), F32),
             pltpu.VMEM((8, HALF), F32),
             pltpu.VMEM((15, 8, 128), F32),
-            pltpu.VMEM((HALF, D), F32),
+            pltpu.VMEM((3 * ROWS, D), F32),
             pltpu.VMEM((8, ROWS, D), BF16),
             pltpu.VMEM((8, ROWS, D), BF16),
             pltpu.VMEM((2, 7, ROWS, D), BF16),
             pltpu.VMEM((2, 7, ROWS, D), BF16),
+            pltpu.VMEM((8, ROWS, D), F32),
+            pltpu.VMEM((ROWS, D), F32),
             dma((2, 11)), dma((2, 11)),
             dma((8,)), dma((8,)),
             dma((15,)), dma((15,)),
             dma((2, 10)), dma((2, 10)),
             dma((8,)), dma((8,)),
             dma((7,)), dma((7,)),
+            dma((6, 5)), dma((6, 5)),
         ],
         compiler_params=pltpu.CompilerParams(
             collective_id=0, has_side_effects=True, vmem_limit_bytes=60 << 20
@@ -422,18 +493,9 @@
     )(log_scale, bias, images, texts, labels)
 
 
-def back(rows, grad):
-    rows = rows.astype(F32)
-    inv = lax.rsqrt(jnp.sum(rows * rows, axis=-1, keepdims=True) + EPS)
-    n = rows * inv
-    return (grad - n * jnp.sum(n * grad, axis=-1, keepdims=True)) * inv
-
-
 def body(images, texts, match, log_scale, bias):
-    labels = jnp.pad(match, (0, 1024 - ROWS)).reshape(8, 128)
-    du, dv, loss = fused(log_scale.reshape(1), bias.reshape(1), images, texts, labels)
-    scale = jnp.exp(log_scale)
-    return (loss[0, 0], back(images, scale * du), back(texts, scale * dv))
+    du, dv, loss = fused(log_scale.reshape(1), bias.reshape(1), images, texts, match.reshape(1, ROWS))
+    return (loss.reshape(()), du, dv)
 
 
 def solution(mesh):

time: 115 us -> 97.3 us (0.85)
  Pallas kernels: 104 us -> 89.9 us
  other arithmetic: 5.45 us -> 0 us
  between operations: 2.07 us -> 3.69 us
    pallas_call x1, Pallas kernels: 104 us -> 89.9 us  [fused(): pl.pallas_call(kernel, out_shape=(block, block, jax.ShapeDtypeStruct((1,)...]
    reduce_sum x3 -> x0, other arithmetic: 3.18 us -> none  [the longest x1 1.86 us: back(): return (grad - n * jnp.sum(n * grad, axis=-1, keepdims=True)) * inv]
    unnamed x12 -> x4, local copies, waits for them, and re-layouts: 0.69 us -> 3.05 us
    mul x2 -> x0, other arithmetic: 2.26 us -> none  [back(): return (grad - n * jnp.sum(n * grad, axis=-1, keepdims=True)) * inv]
    slice x1 -> x0, local copies, waits for them, and re-layouts: 1.19 us -> none  [body(): return (loss[0, 0], back(images, scale * du), back(texts, scale * dv))]
where the time goes in v2:
time: 97.3 us; the launch traced here: 96.6 us
  Pallas kernels  89.9 us (92%)
  between operations  3.69 us (4%)
  local copies, waits for them, and re-layouts  3.05 us (3%)
    pallas_call x1, Pallas kernels, fused(): pl.pallas_call(kernel, out_shape=(block, block, jax.ShapeDtypeStruct((1,)...  89.9 us
    unnamed x4, local copies, waits for them, and re-layouts  3.05 us

profile of v2, /device:TPU:1, one launch (start us, length us, event | category | flops | bytes accessed | tf_op | source)
XLA Modules:
  0.0 96.6 jit_solution(10024579401305987798)
XLA Ops:
  1.9 89.9 %contrastive.1 = (f32[176,1152]{1,0:T(8,128)}, f32[176,1152]{1,0:T(8,128)}, f32[1]{0:T(128)}) custom-call(f32[1]{0:T(128)} %bitcast.4.ls_ref, f32[1]{0:T(128)} %bitcast.5.bias_ref, bf16[176,1152]{1,0:T(8,128)(2,1)} %img_ref.1, bf16[176,1152]{1,0:T(8,128)(2,1)} %txt_ref.1, s32[1,176]{1,0:T(1,128)} %bitcast.6), custom_call_target="tpu_custom_call" | custom-call | tf_op jit(solution)/shard_map/contrastive/pallas_call | solution.py:460
  92.4 0.0 copy-start
  92.4 2.2 %copy.14 = f32[176,1152]{1,0:T(8,128)} copy(f32[176,1152]{1,0:T(8,128)} %get-tuple-element.13) | data formatting | bytes 1622016
  94.6 0.0 copy-done
  94.6 0.9 copy.15
Async XLA Ops:
  92.4 2.2 %copy-start = (f32[176,1152]{1,0:T(8,128)S(1)}, f32[176,1152]{1,0:T(8,128)}, u32[]{:S(2)}) copy-start(f32[176,1152]{1,0:T(8,128)} %get-tuple-element.14) | copy-start | bytes 2433028

commit v3 on v2

--- a/solution.py
+++ b/solution.py
@@ -31,6 +31,9 @@
     return 352 * PLACE[k] + ROWS
 
 
+EARLY = other_row(4)
+
+
 def nt(a, b):
     return lax.dot_general(a, b, (((1,), (1,)), ((), ())), preferred_element_type=F32)
 
@@ -48,7 +51,7 @@
     du_ref, dv_ref, loss_ref,
     u, v, g0, g1, labs, labb, acc, lossbuf,
     dvf, core_out, core_in, stage, recv,
-    own, dvt, gs, gr, cs, cr, lsend, lrecv, rs, rr, ccs, ccr, ps, pr, ts, tr,
+    own, pdu, dvt, gs, gr, cs, cr, lsend, lrecv, rs, rr, ccs, ccr, ps, pr, ts, tr,
 ):
     im = lax.axis_index("img")
     tx = lax.axis_index("txt")
@@ -113,12 +116,16 @@
         (0, 2, CUT, ROWS - CUT, minus),
         (0, 2, 0, CUT, minus),
         (0, 3, 0, ROWS, part),
-        (1, 4, 0, CUT, plus),
-        (2, 4, CUT, ROWS - CUT, minus),
+        (1, 4, 0, 48, plus),
+        (2, 4, 96, 48, minus),
         (3, 5, 0, ROWS, plus),
         (3, 6, 0, ROWS, minus),
-        (4, 7, 0, CUT, part),
-        (4, 7, CUT, ROWS - CUT, part),
+        (1, 4, 48, 48, plus),
+        (2, 4, 144, 32, minus),
+        (4, 7, 0, 48, part),
+        (4, 7, 96, 48, part),
+        (4, 7, 48, 48, part),
+        (4, 7, 144, 32, part),
     )
 
     def gcopy(f, i):
@@ -184,8 +191,10 @@
 
     gwait(0)
     gstart(5)
+    gstart(9)
     gwait(2)
     gstart(6)
+    gstart(10)
     for n, (d, slot) in enumerate(group):
         copy(labs.at[2 * PLACE[0] + 1], labs.at[slot], lsend.at[n], lrecv.at[n], d).wait_recv()
     bases = []
@@ -213,31 +222,46 @@
         start(xcopy(k))
     xcopy(0).wait_recv()
     logits_span(PLACE[0], 1, 0)
+    gwait(5)
+    gstart(11)
+    gwait(6)
+    gstart(12)
     for k in (1, 2, 3):
         xcopy(k).wait_recv()
-    logits_span(PLACE[3], 1, 0)
-    gwait(5)
-    gstart(9)
-    gwait(6)
-    gstart(10)
+    logits_span(PLACE[3], 2, 0)
+    gwait(9)
+    gstart(13)
+    gwait(10)
+    gstart(14)
     start(xcopy(4))
-    logits_span(PLACE[1], 2, 0)
+    logits_span(PLACE[2], 1, 0)
     xcopy(4).wait_recv()
     logits_span(PLACE[4], 1, 0)
+
+    @pl.loop(0, 4 * one)
+    def _(i):
+        at = pl.multiple_of(i * 352, 16)
+        pdu[pl.ds(at, 352), :] = nn(g0[pl.ds(same_row(4) + at, 352), :], v[0:HALF, :])
+
+    @pl.loop(0, one)
+    def _(_i):
+        pdu[8 * ROWS :, :] = nn(g0[same_row(0) :, :], v[0:HALF, :])
+
     gwait(7)
     start(xcopy(5))
     gwait(8)
     start(xcopy(6))
     xcopy(5).wait_recv()
     logits_span(PLACE[5], 1, 0)
-    gwait(9)
-    gwait(10)
+    for i in (11, 12, 13, 14):
+        gwait(i)
     start(xcopy(7))
+    logits_span(PLACE[4], 5, 1)
     xcopy(6).wait_recv()
     logits_span(PLACE[6], 1, 0)
     xcopy(7).wait_recv()
     logits_span(PLACE[7], 1, 0)
-    logits_span(0, 8, 1)
+    logits_span(0, 3, 1)
 
     mine = jnp.broadcast_to(jnp.sum(acc[...]).reshape(1, 1), (8, 128))
     lossbuf[0] = mine
@@ -257,7 +281,8 @@
     start(pcopy(0))
 
     rmoves = (
-        (7, 7, 0, ROWS, part),
+        (7, 7, 0, CUT, part),
+        (7, 7, CUT, ROWS - CUT, part),
         (5, 5, 0, ROWS, minus),
         (6, 6, 0, ROWS, plus),
         (4, 4, 0, CUT, minus),
@@ -268,7 +293,7 @@
         (2, 2, CUT, ROWS - CUT, plus),
         (3, 3, 0, ROWS, part),
     )
-    S7, S5, S6, S4A, S4B, S1A, S1B, S2A, S2B, S3 = range(10)
+    S7A, S7B, S5, S6, S4A, S4B, S1A, S1B, S2A, S2B, S3 = range(11)
 
     def rcopy(f, i):
         k, _, lo, n, to = rmoves[i]
@@ -290,9 +315,15 @@
             first = other_row(nxt) if k is None else same_row(k)
             n = ROWS if k is None or nxt is None else 352
             rows = pl.ds(first, n)
-            d = nn(g0[rows, :], v[0:HALF, :]) + nn(g1[rows, :], v[HALF:, :])
-            if k is not None:
-                own[k] = d[:ROWS]
+            d = nn(g1[rows, :], v[HALF:, :])
+            if k in (None, 5, 6, 7):
+                d = d + nn(g0[rows, :], v[0:HALF, :])
+                if k is not None:
+                    own[k - 5] = d[:ROWS]
+            else:
+                at = first - same_row(4)
+                d = d + pdu[at : at + n, :]
+                pdu[at : at + ROWS, :] = d[:ROWS]
             if nxt is not None:
                 core_out[nxt] = d[n - ROWS :].astype(BF16)
 
@@ -309,8 +340,10 @@
         (3, 0, ROWS, part),
         (1, CUT, ROWS - CUT, minus),
         (2, 0, CUT, plus),
+        (4, 0, CUT, minus),
+        (4, CUT, ROWS - CUT, plus),
     )
-    T7, T5, T6, T3, T1B, T2A = range(6)
+    T7, T5, T6, T3, T1B, T2A, T4A, T4B = range(8)
 
     def tcopy(i, n):
         k, lo, rows, to = tmoves[i]
@@ -323,7 +356,7 @@
         for n in range(5):
             tcopy(i, n).wait_recv()
 
-    def dv_late(n):
+    def dv_late(n, step=None):
         cols = tcols(n)
 
         @pl.loop(0, one)
@@ -333,6 +366,8 @@
             for k in (5, 6, 7):
                 stage[1, k - 1, :, cols] = d[(k - 4) * ROWS : (k - 3) * ROWS].astype(BF16)
 
+        if step is not None:
+            pnext(step)
         for i in (T7, T5, T6):
             start(tcopy(i, n))
 
@@ -344,7 +379,7 @@
         @pl.loop(0, one)
         def _(_i):
             d = tn(g0[...], u[:, cols])
-            dvf[:, cols] = d[0 : 3 * ROWS]
+            dvf[0 : 3 * ROWS, cols] = d[0 : 3 * ROWS]
             stage[1, 0, CUT:, cols] = d[ROWS + CUT : 2 * ROWS].astype(BF16)
             stage[1, 1, 0:CUT, cols] = d[2 * ROWS : 2 * ROWS + CUT].astype(BF16)
             both = recv[1, 4, :, cols].astype(F32) + recv[1, 5, :, cols].astype(F32)
@@ -354,62 +389,73 @@
             start(tcopy(i, n))
 
     def mine_of(k, lo=0, n=ROWS):
-        return own[k, lo : lo + n, :] + core_in[k, lo : lo + n, :].astype(F32)
+        if k >= 5:
+            mine = own[k - 5, lo : lo + n, :]
+        else:
+            at = same_row(k) - same_row(4) + lo
+            mine = pdu[at : at + n, :]
+        return mine + core_in[k, lo : lo + n, :].astype(F32)
 
     du_block(None, 7)
-    dv_late(0)
-    pnext(0)
+    dv_late(0, 0)
     du_block(7, 5)
     ccopy(7).wait_recv()
     put(0, 7, mine_of(7))
-    start(rcopy(0, S7))
-    dv_late(1)
-    pnext(1)
+    start(rcopy(0, S7A))
+    start(rcopy(0, S7B))
     du_block(5, 6)
     ccopy(5).wait_recv()
     put(0, 5, mine_of(5))
+    pnext(1)
     start(rcopy(0, S5))
-    dv_late(2)
-    pnext(2)
     du_block(6, 4)
     ccopy(6).wait_recv()
     put(0, 6, mine_of(6))
     start(rcopy(0, S6))
+    dv_late(1, 2)
+    dv_late(2)
     dv_late(3)
-    pnext(3)
-    dv_late(4)
-    pnext(4)
+    dv_late(4, 3)
     du_block(4, 3)
+
+    ccopy(4).wait_recv()
+    rcopy(0, S7A).wait_recv()
+    put(0, 4, mine_of(4, 0, CUT) + got(0, 7, 0, CUT), 0, CUT)
+    start(rcopy(0, S4A))
     du_block(3, 1)
-    pnext(5)
-
-    ccopy(4).wait_recv()
-    rcopy(0, S7).wait_recv()
-    put(0, 4, mine_of(4) + got(0, 7))
-    start(rcopy(0, S4A))
+    rcopy(0, S7B).wait_recv()
+    put(0, 4, mine_of(4, CUT, ROWS - CUT) + got(0, 7, CUT, ROWS - CUT), CUT, ROWS - CUT)
     start(rcopy(0, S4B))
-    twait(T7)
-    put(1, 4, dvt[...] + got(1, 7))
-    start(rcopy(1, S4A))
-    start(rcopy(1, S4B))
-    pnext(6)
-
+
+    def text_four(n):
+        cols = tcols(n)
+        tcopy(T7, n).wait_recv()
+        stage[1, 3, :, cols] = (dvt[:, cols] + recv[1, 6, :, cols].astype(F32)).astype(BF16)
+        start(tcopy(T4A, n))
+        start(tcopy(T4B, n))
+
+    text_four(0)
+    text_four(1)
     dv_early(0)
+    text_four(2)
     du_block(1, 2)
     ccopy(1).wait_recv()
     put(0, 1, mine_of(1, CUT, ROWS - CUT), CUT, ROWS - CUT)
     start(rcopy(0, S1B))
+    text_four(3)
     dv_early(1)
+    text_four(4)
     ccopy(3).wait_recv()
     rcopy(0, S5).wait_recv()
     rcopy(0, S6).wait_recv()
     put(0, 3, mine_of(3) + got(0, 5) + got(0, 6))
+    pnext(4)
     start(rcopy(0, S3))
+    dv_early(2)
     du_block(2, 0)
     ccopy(2).wait_recv()
     put(0, 2, mine_of(2, 0, CUT), 0, CUT)
     start(rcopy(0, S2A))
-    dv_early(2)
     dv_early(3)
 
     rcopy(0, S4A).wait_recv()
@@ -419,34 +465,38 @@
     put(0, 2, mine_of(2, CUT, ROWS - CUT) + got(0, 4, CUT, ROWS - CUT), CUT, ROWS - CUT)
     start(rcopy(0, S2B))
     dv_early(4)
-    rcopy(1, S4A).wait_recv()
+    pnext(5)
+    du_block(0, None)
+    twait(T4A)
     put(1, 1, dvf[ROWS : ROWS + CUT, :] + got(1, 4, 0, CUT), 0, CUT)
     start(rcopy(1, S1A))
-    rcopy(1, S4B).wait_recv()
+    twait(T4B)
     put(1, 2, dvf[2 * ROWS + CUT : 3 * ROWS, :] + got(1, 4, CUT, ROWS - CUT), CUT, ROWS - CUT)
     start(rcopy(1, S2B))
-    du_block(0, None)
 
     ccopy(0).wait_recv()
+
+    def finish(f, ref, out, grad, lo, n):
+        rows = ref[lo : lo + n, :].astype(F32)
+        inv = lax.rsqrt(jnp.sum(rows * rows, axis=-1, keepdims=True) + EPS)
+        unit = rows * inv
+        grad = (grad + got(f, 1, lo, n) + got(f, 2, lo, n) + got(f, 3, lo, n)) * scale[0:1, 0:1]
+        out[lo : lo + n, :] = (grad - unit * jnp.sum(unit * grad, axis=-1, keepdims=True)) * inv
+
+    rest = ROWS - CUT
+    for i in (S1B, S2A, S3, S1A):
+        rcopy(0, i).wait_recv()
+    finish(0, img_ref, du_ref, mine_of(0, 0, CUT), 0, CUT)
+    for i in (T3, T1B, T2A):
+        twait(i)
+    rcopy(1, S1A).wait_recv()
+    finish(1, txt_ref, dv_ref, dvf[0:CUT, :], 0, CUT)
+    rcopy(0, S2B).wait_recv()
+    finish(0, img_ref, du_ref, mine_of(0, CUT, rest), CUT, rest)
+    rcopy(1, S2B).wait_recv()
+    finish(1, txt_ref, dv_ref, dvf[CUT:ROWS, :], CUT, rest)
+    pnext(6)
     loss_ref[0] = jnp.max(lossbuf[14]) * (LN2 / BATCH)
-
-    def finish(f, ref, out, grad):
-        rows = ref[...].astype(F32)
-        inv = lax.rsqrt(jnp.sum(rows * rows, axis=-1, keepdims=True) + EPS)
-        n = rows * inv
-        if f == 0:
-            for i in (S1A, S1B, S2A, S2B, S3):
-                rcopy(0, i).wait_recv()
-        else:
-            for i in (S1A, S2B):
-                rcopy(1, i).wait_recv()
-            for i in (T3, T1B, T2A):
-                twait(i)
-        grad = (grad + got(f, 1) + got(f, 2) + got(f, 3)) * scale[0:1, 0:1]
-        out[...] = (grad - n * jnp.sum(n * grad, axis=-1, keepdims=True)) * inv
-
-    finish(0, img_ref, du_ref, mine_of(0))
-    finish(1, txt_ref, dv_ref, dvf[0:ROWS, :])
 
     for cp in sent:
         cp.wait_send()
@@ -456,7 +506,7 @@
     vm = pl.BlockSpec(memory_space=pltpu.VMEM)
     sm = pl.BlockSpec(memory_space=pltpu.SMEM)
     dma = pltpu.SemaphoreType.DMA
-    block = jax.ShapeDtypeStruct((ROWS, D), F32)
+    block = pltpu.VMEM((ROWS, D), F32)
     return pl.pallas_call(
         kernel,
         out_shape=(block, block, jax.ShapeDtypeStruct((1,), F32)),
@@ -471,20 +521,21 @@
             pltpu.VMEM((16 * ROWS, 128), F32),
             pltpu.VMEM((8, HALF), F32),
             pltpu.VMEM((15, 8, 128), F32),
-            pltpu.VMEM((3 * ROWS, D), F32),
+            pltpu.VMEM((HALF, D), F32),
             pltpu.VMEM((8, ROWS, D), BF16),
             pltpu.VMEM((8, ROWS, D), BF16),
             pltpu.VMEM((2, 7, ROWS, D), BF16),
             pltpu.VMEM((2, 7, ROWS, D), BF16),
-            pltpu.VMEM((8, ROWS, D), F32),
+            pltpu.VMEM((3, ROWS, D), F32),
+            pltpu.VMEM((9 * ROWS, D), F32),
             pltpu.VMEM((ROWS, D), F32),
+            dma((2, 15)), dma((2, 15)),
+            dma((8,)), dma((8,)),
+            dma((15,)), dma((15,)),
             dma((2, 11)), dma((2, 11)),
             dma((8,)), dma((8,)),
-            dma((15,)), dma((15,)),
-            dma((2, 10)), dma((2, 10)),
-            dma((8,)), dma((8,)),
             dma((7,)), dma((7,)),
-            dma((6, 5)), dma((6, 5)),
+            dma((8, 5)), dma((8, 5)),
         ],
         compiler_params=pltpu.CompilerParams(
             collective_id=0, has_side_effects=True, vmem_limit_bytes=60 << 20

time: 97.3 us -> 88.2 us (0.906)
  Pallas kernels: 89.9 us -> 82.6 us
  local copies, waits for them, and re-layouts: 3.05 us -> 1.78 us
    pallas_call x1, Pallas kernels: 89.9 us -> 82.6 us  [fused(): pl.pallas_call(kernel, out_shape=(block, block, jax.ShapeDtypeStruct((1,)...]
    unnamed x4 -> x2, local copies, waits for them, and re-layouts: 3.05 us -> 1.78 us
where the time goes in v3:
time: 88.2 us; the launch traced here: 88 us
  Pallas kernels  82.6 us (94%)
  between operations  3.62 us (4%)
  local copies, waits for them, and re-layouts  1.78 us (2%)
    pallas_call x1, Pallas kernels, fused(): pl.pallas_call(kernel, out_shape=(block, block, jax.ShapeDtypeStruct((1,)...  82.6 us
    unnamed x2, local copies, waits for them, and re-layouts  1.78 us

profile of v3, /device:TPU:1, one launch (start us, length us, event | category | flops | bytes accessed | tf_op | source)
XLA Modules:
  0.0 88.0 jit_solution(3776651999778653144)
XLA Ops:
  1.9 82.6 %contrastive.1 = (f32[176,1152]{1,0:T(8,128)S(1)}, f32[176,1152]{1,0:T(8,128)S(1)}, f32[1]{0:T(128)}) custom-call(f32[1]{0:T(128)} %bitcast.4.ls_ref, f32[1]{0:T(128)} %bitcast.5.bias_ref, bf16[176,1152]{1,0:T(8,128)(2,1)} %img_ref.1, bf16[176,1152]{1,0:T(8,128)(2,1)} %txt_ref.1, s32[1,176]{1,0:T(1,128)} %bitcast.6), custom_call_target="tpu_custom_call" | custom-call | tf_op jit(solution)/shard_map/contrastive/pallas_call | solution.py:510
  84.6 0.9 %copy.11 = f32[176,1152]{1,0:T(8,128)} copy(f32[176,1152]{1,0:T(8,128)S(1)} %get-tuple-element.10) | data formatting | bytes 1622016
  85.4 0.9 %copy.12 = f32[176,1152]{1,0:T(8,128)} copy(f32[176,1152]{1,0:T(8,128)S(1)} %get-tuple-element.11) | data formatting | bytes 1622016
